TPU v7x, 32 devices: a whole 2x2x4 slice. The times are simulated.
32 devices in a mesh: groups: 2 (over y), tensor: 4 (over z), dp: 4 (over x, core).
Axes of the slice: x: 2, y: 2, z: 4, core: 2. Of those that a mesh axis runs over, the one named last changes fastest.
Arguments:
- incoming_entries: bfloat16 [256, 4608], P(('groups', 'tensor'), 'dp'), parts along dimension 0, may hold values from -6 to 6
- output_adjoint: bfloat16 [256, 4608], P(('groups', 'tensor'), 'dp'), parts along dimension 0, may hold values from -1.5 to 1.5
- remaining_members: int32 [3], replicated, may hold values from 0 to 3, as said below
- gating_matrix: bfloat16 [4608, 18432], P('dp', 'tensor'), may hold values from -0.09375 to 0.09375
- expansion_matrix: bfloat16 [4608, 18432], P('dp', 'tensor'), may hold values from -0.09375 to 0.09375
- contraction_matrix: bfloat16 [18432, 4608], P('tensor', 'dp'), may hold values from -0.046875 to 0.046875
Outputs:
- grad_tokens: bfloat16 [256, 4608], P(('groups', 'tensor'), 'dp'), parts along dimension 0
- grad_gate: bfloat16 [9216, 18432], P(('groups', 'dp'), 'tensor'), parts along dimension 0
- grad_up: bfloat16 [9216, 18432], P(('groups', 'dp'), 'tensor'), parts along dimension 0
- grad_down: bfloat16 [36864, 4608], P(('groups', 'tensor'), 'dp'), parts along dimension 0
There are 2 independent parts, one for each index of `groups`. A program takes and returns all parts, laid end to end along the dimension named above; an argument that names none is the same for every part. Nothing has to cross between parts.
Inputs may be any that keep to these rules, and one draw needn't show every extreme that they name: `remaining_members`: 3 distinct ranks of the tensor axis, rank 0 and rank 4 - 1 among them; the hidden units of the other ranks' blocks are switched off.
All inputs are finite; a program needn't handle non-finite values.
Results may differ from a plain program's by a relative error of at most 0.02.
Values may be sent and summed in bfloat16 or wider, within the bound.
A program may use at most 192 MiB of HBM per device.

v0:
```python
import math

import jax
import jax.numpy as jnp
from jax import lax
from jax.sharding import PartitionSpec as P

cubic_coef = 0.044715


def gelu_pair(pre_act):
    tanh_scale = math.sqrt(2.0 / math.pi)
    tangent = jnp.tanh(tanh_scale * (pre_act + cubic_coef * pre_act * pre_act * pre_act))
    active = 0.5 * pre_act * (1.0 + tangent)
    slope_val = 0.5 * (1.0 + tangent) + 0.5 * pre_act * (1.0 - tangent * tangent) * tanh_scale * (
        1.0 + 3.0 * cubic_coef * pre_act * pre_act
    )
    return (active, slope_val)


def activate(totals, retained_marker):
    gate_sum = totals[:, 0]
    up_sum = totals[:, 1]
    back_sum = totals[:, 2]
    active, slope_val = gelu_pair(gate_sum)
    hidden = (retained_marker * active * up_sum).astype(jnp.bfloat16)
    gate_grad = (retained_marker * back_sum * up_sum * slope_val).astype(jnp.bfloat16)
    up_grad = (retained_marker * back_sum * active).astype(jnp.bfloat16)
    return (hidden, gate_grad, up_grad)


def body(
    incoming_entries,
    output_adjoint,
    remaining_members,
    gating_matrix,
    expansion_matrix,
    contraction_matrix,
):
    cycle_location = lax.axis_index("tensor")
    retained_marker = jnp.sum((remaining_members == cycle_location).astype(jnp.float32))
    tok_all, cot_all = (
        lax.all_gather(incoming_entries, "tensor", axis=0, tiled=True),
        lax.all_gather(output_adjoint, "tensor", axis=0, tiled=True),
    )
    gate_part = jnp.dot(tok_all, gating_matrix, preferred_element_type=jnp.float32)
    up_part = jnp.dot(tok_all, expansion_matrix, preferred_element_type=jnp.float32)
    back_part = lax.dot_general(
        cot_all, contraction_matrix, (((1,), (1,)), ((), ())), preferred_element_type=jnp.float32
    )
    totals = lax.psum_scatter(
        jnp.stack([gate_part, up_part, back_part], axis=1).astype(jnp.bfloat16),
        "dp",
        scatter_dimension=0,
        tiled=True,
    ).astype(jnp.float32)
    hidden_loc, gate_loc, up_loc = activate(totals, retained_marker)
    hidden, gate_grad, up_grad = (
        lax.all_gather(hidden_loc, "dp", axis=0, tiled=True),
        lax.all_gather(gate_loc, "dp", axis=0, tiled=True),
        lax.all_gather(up_loc, "dp", axis=0, tiled=True),
    )
    over_rows = (((0,), (0,)), ((), ()))
    grad_gate = lax.dot_general(
        tok_all, gate_grad, over_rows, preferred_element_type=jnp.float32
    ).astype(jnp.bfloat16)
    grad_up = lax.dot_general(
        tok_all, up_grad, over_rows, preferred_element_type=jnp.float32
    ).astype(jnp.bfloat16)
    grad_down = lax.dot_general(
        hidden, cot_all, over_rows, preferred_element_type=jnp.float32
    ).astype(jnp.bfloat16)
    over_units = (((1,), (1,)), ((), ()))
    first = lax.dot_general(
        gate_grad, gating_matrix, over_units, preferred_element_type=jnp.float32
    )
    second = lax.dot_general(
        up_grad, expansion_matrix, over_units, preferred_element_type=jnp.float32
    )
    grad_tokens = lax.psum_scatter(
        (first + second).astype(jnp.bfloat16), "tensor", scatter_dimension=0, tiled=True
    )
    return (grad_tokens, grad_gate, grad_up, grad_down)


def solution(mesh):
    return jax.shard_map(
        body,
        mesh=mesh,
        in_specs=(
            P(("groups", "tensor"), "dp"),
            P(("groups", "tensor"), "dp"),
            P(),
            P("dp", "tensor"),
            P("dp", "tensor"),
            P("tensor", "dp"),
        ),
        out_specs=(
            P(("groups", "tensor"), "dp"),
            P(("groups", "dp"), "tensor"),
            P(("groups", "dp"), "tensor"),
            P(("groups", "tensor"), "dp"),
        ),
        check_vma=False,
    )
```

profile of v0, /device:TPU:0, one launch (start us, length us, event | category | flops | bytes accessed | tf_op | source)
XLA Modules:
  0.0 199.9 jit_solution(13395023645945512084)
XLA Ops:
  7.2 0.0 reduce-scatter.3.cloned.1.call-start
  7.2 15.9 %all_gather.15 = bf16[128,1152]{1,0:T(8,128)(2,1)S(1)} all-gather(bf16[32,1152]{1,0:T(8,128)(2,1)} %param.6), channel_id=1, replica_groups=mesh['groups'=2,'tensor'=4,'dp'=4] {'tensor'}, dimensions={0}, use_global_device_ids=true | all-gather | bytes 368640 | tf_op jit(solution)/shard_map/all_gather | solution.py:43
  23.1 5.9 %fusion.2 = bf16[128,1,4608]{2,0,1:T(8,128)(2,1)S(1)} fusion(bf16[128,1152]{1,0:T(8,128)(2,1)S(1)} %all_gather.15, bf16[1152,4608]{1,0:T(8,128)(2,1)} %param.9), kind=kOutput, calls=%fused_computation.8 | convolution fusion | flops 1359544320 | bytes 12091392 | tf_op jit(solution)/shard_map/dot_general | solution.py:46
  28.9 1.2 copy-done
  30.1 1.7 fusion.3
  31.8 15.0 %all_gather.16 = bf16[128,1152]{1,0:T(8,128)(2,1)S(1)} all-gather(bf16[32,1152]{1,0:T(8,128)(2,1)S(1)} %copy-done.3), channel_id=1, replica_groups=mesh['groups'=2,'tensor'=4,'dp'=4] {'tensor'}, dimensions={0}, use_global_device_ids=true | all-gather | bytes 368640 | tf_op jit(solution)/shard_map/all_gather | solution.py:44
  46.9 3.5 %fusion.4 = bf16[128,1,4608]{2,0,1:T(8,128)(2,1)S(1)} fusion(bf16[128,1152]{1,0:T(8,128)(2,1)S(1)} %all_gather.16, bf16[4608,1152]{1,0:T(8,128)(2,1)S(1)} %bitcast.49), kind=kOutput, calls=%fused_computation.10 | convolution fusion | flops 1359544320 | bytes 12091392 | tf_op jit(solution)/shard_map/dot_general | solution.py:48
  50.4 2.0 %pad_maximum_fusion = bf16[128,3,4608]{2,0,1:T(8,128)(2,1)} fusion(bf16[128,1,4608]{2,0,1:T(8,128)(2,1)S(1)} %fusion.4, bf16[128,1,4608]{2,0,1:T(8,128)(2,1)S(1)} %fusion.3, bf16[128,1,4608]{2,0,1:T(8,128)(2,1)S(1)} %fusion.2), kind=kLoop, calls=%fused_computation.11 | loop fusion | flops 3538944 | bytes 7077888 | tf_op jit(solution)/shard_map/stack | solution.py:52
  52.4 0.0 reduce-scatter.3.cloned.1.call-update
  52.4 0.0 all-gather.4.cloned.1.call-start
  52.4 0.6 copy-done.4
  53.0 0.6 fusion.14
  53.6 40.2 %reduce-scatter.3.cloned.1.call-done = bf16[32,3,4608]{2,0,1:T(8,128)(2,1)} async-done(((bf16[128,3,4608]{2,0,1:T(8,128)(2,1)}), bf16[32,3,4608]{2,0,1:T(8,128)(2,1)}) %reduce-scatter.3.cloned.1.call-update) | async-done | bytes 884752 | tf_op jit(solution)/shard_map/reduce_scatter | solution.py:51
  93.8 1.3 convert_element_type.35
  95.2 2.1 %multiply_convert_fusion = (bf16[32,4608]{1,0:T(8,128)(2,1)}, bf16[32,4608]{1,0:T(8,128)(2,1)}, bf16[32,4608]{1,0:T(8,128)(2,1)}) fusion(f32[32,3,4608]{2,0,1:T(8,128)S(1)} %convert_element_type.35, f32[]{:T(128)} %fusion.14), kind=kLoop, calls=%fused_computation.27 | loop fusion | flops 3981312 | bytes 2655232 | tf_op jit(solution)/shard_map/convert_element_type | solution.py:26
  97.3 0.0 all-gather.4.cloned.1.call-update
  97.3 0.0 all-gather.6.cloned.1.call-start
  97.3 0.7 all-gather.6.cloned.1.call-update
  98.0 0.0 all-gather.8.cloned.1.call-start
  98.1 0.5 all-gather.8.cloned.1.call-update
  98.6 0.2 reduce-scatter.5.cloned.1.call-start
  98.8 16.1 %all-gather.4.cloned.1.call-done = bf16[128,4608]{1,0:T(8,128)(2,1)} async-done(((bf16[32,4608]{1,0:T(8,128)(2,1)}), bf16[128,4608]{1,0:T(8,128)(2,1)}) %all-gather.4.cloned.1.call-update) | async-done | bytes 1179664 | tf_op jit(solution)/shard_map/all_gather | solution.py:60
  114.9 7.8 %fusion.15 = f32[128,1152]{1,0:T(8,128)S(1)} fusion(bf16[128,4608]{1,0:T(8,128)(2,1)} %all-gather.4.cloned.1.call-done, bf16[1152,4608]{1,0:T(8,128)(2,1)} %param.9), kind=kOutput, calls=%fused_computation.32 | convolution fusion | flops 1358954496 | bytes 12386304 | tf_op jit(solution)/shard_map/dot_general | solution.py:74
  122.7 11.9 %all-gather.6.cloned.1.call-done = bf16[128,4608]{1,0:T(8,128)(2,1)} async-done(((bf16[32,4608]{1,0:T(8,128)(2,1)}), bf16[128,4608]{1,0:T(8,128)(2,1)}) %all-gather.6.cloned.1.call-update) | async-done | bytes 1179664 | tf_op jit(solution)/shard_map/all_gather | solution.py:61
  134.6 8.5 %fusion.5 = bf16[128,1152]{1,0:T(8,128)(2,1)} fusion(f32[128,1152]{1,0:T(8,128)S(1)} %fusion.15, bf16[128,4608]{1,0:T(8,128)(2,1)} %all-gather.6.cloned.1.call-done, bf16[1152,4608]{1,0:T(8,128)(2,1)} %param.10), kind=kOutput, calls=%fused_computation.13 | convolution fusion | flops 1359249408 | bytes 12681216 | tf_op jit(solution)/shard_map/dot_general | solution.py:77
  143.1 0.0 reduce-scatter.5.cloned.1.call-update
  143.2 0.0 copy-done.1
  143.2 5.7 %fusion = bf16[1152,4608]{0,1:T(8,128)(2,1)} fusion(bf16[128,4608]{1,0:T(8,128)(2,1)S(1)} %copy-done.1, bf16[128,1152]{1,0:T(8,128)(2,1)S(1)} %all_gather.15), kind=kOutput, calls=%fused_computation.3 | convolution fusion | flops 1364262912 | bytes 12091392 | tf_op jit(solution)/shard_map/dot_general | solution.py:64
  148.9 5.7 %fusion.1 = bf16[1152,4608]{0,1:T(8,128)(2,1)} fusion(bf16[128,4608]{1,0:T(8,128)(2,1)S(1)} %copy-done.2, bf16[128,1152]{1,0:T(8,128)(2,1)S(1)} %all_gather.15), kind=kOutput, calls=%fused_computation.4 | convolution fusion | flops 1364262912 | bytes 12091392 | tf_op jit(solution)/shard_map/dot_general | solution.py:67
  154.6 15.2 %copy.10 = bf16[1152,4608]{1,0:T(8,128)(2,1)} copy(bf16[1152,4608]{0,1:T(8,128)(2,1)} %fusion) | data formatting | bytes 21233664
  169.8 15.2 %copy.11 = bf16[1152,4608]{1,0:T(8,128)(2,1)} copy(bf16[1152,4608]{0,1:T(8,128)(2,1)} %fusion.1) | data formatting | bytes 21233664
  185.0 8.4 %convolution_convert_fusion = bf16[4608,1152]{1,0:T(8,128)(2,1)} fusion(bf16[128,4608]{1,0:T(8,128)(2,1)} %all-gather.8.cloned.1.call-done, bf16[128,1152]{1,0:T(8,128)(2,1)S(1)} %all_gather.16), kind=kOutput, calls=%fused_computation | convolution fusion | flops 1364262912 | bytes 12091392 | tf_op jit(solution)/shard_map/dot_general | solution.py:70
  (16 shorter events, 0.0 us)
Async XLA Ops:
  7.2 86.7 %reduce-scatter.3.cloned.1.call-start = ((), (), s32[]{:S(2)}) async-start(), calls=%async_computation.2 | async-start | bytes 4423680 | tf_op jit(solution)/shard_map/reduce_scatter | solution.py:51
  23.1 7.0 %copy-start = (bf16[1152,4608]{1,0:T(8,128)(2,1)S(1)}, bf16[1152,4608]{1,0:T(8,128)(2,1)}, u32[]{:S(2)}) copy-start(bf16[1152,4608]{1,0:T(8,128)(2,1)} %param.10) | copy-start | bytes 31850500
  23.1 23.8 %slice-start = ((s8[10616832]{0:T(1024)(128)(4,1)}), s8[4194304]{0:T(1024)(128)(4,1)S(1)}, s32[]{:S(2)}) async-start(s8[10616832]{0:T(1024)(128)(4,1)} %bitcast.48), calls=%async_computation.7 | async-start | bytes 8388608
  23.1 23.8 %slice-start.1 = ((s8[10616832]{0:T(1024)(128)(4,1)}), s8[4194304]{0:T(1024)(128)(4,1)S(1)}, s32[]{:S(2)}) async-start(s8[10616832]{0:T(1024)(128)(4,1)} %bitcast.48), calls=%async_computation.8 | async-start | bytes 8388608
  30.1 1.7 copy-start.3
  30.1 16.7 %slice-start.2 = ((s8[10616832]{0:T(1024)(128)(4,1)}), s8[2228224]{0:T(1024)(128)(4,1)S(1)}, s32[]{:S(2)}) async-start(s8[10616832]{0:T(1024)(128)(4,1)} %bitcast.48), calls=%async_computation.9 | async-start | bytes 4456448
  52.4 0.7 copy-start.4
  52.4 62.5 %all-gather.4.cloned.1.call-start = ((), (), s32[]{:S(2)}) async-start(), calls=%async_computation.3 | async-start | bytes 1474560 | tf_op jit(solution)/shard_map/all_gather | solution.py:60
  97.3 37.3 %all-gather.6.cloned.1.call-start = ((), (), s32[]{:S(2)}) async-start(), calls=%async_computation.4 | async-start | bytes 1474560 | tf_op jit(solution)/shard_map/all_gather | solution.py:61
  98.0 87.0 %all-gather.8.cloned.1.call-start = ((), (), s32[]{:S(2)}) async-start(), calls=%async_computation.6 | async-start | bytes 1474560 | tf_op jit(solution)/shard_map/all_gather | solution.py:59
  98.6 94.8 %reduce-scatter.5.cloned.1.call-start = ((), (), s32[]{:S(2)}) async-start(), calls=%async_computation.5 | async-start | bytes 368640 | tf_op jit(solution)/shard_map/reduce_scatter | solution.py:80
  122.7 20.4 %copy-start.1 = (bf16[128,4608]{1,0:T(8,128)(2,1)S(1)}, bf16[128,4608]{1,0:T(8,128)(2,1)}, u32[]{:S(2)}) copy-start(bf16[128,4608]{1,0:T(8,128)(2,1)} %all-gather.4.cloned.1.call-done) | copy-start | bytes 3538948
  143.2 5.7 %copy-start.2 = (bf16[128,4608]{1,0:T(8,128)(2,1)S(1)}, bf16[128,4608]{1,0:T(8,128)(2,1)}, u32[]{:S(2)}) copy-start(bf16[128,4608]{1,0:T(8,128)(2,1)} %all-gather.6.cloned.1.call-done) | copy-start | bytes 3538948
Sparse Core Ops, SparseCore 0:
  52.5 41.2 reduce-scatter.2
  97.4 17.4 all-gather.3
  117.1 17.4 all-gather.5
  136.1 17.4 all-gather.7
  156.4 19.8 reduce-scatter.4
where the time goes:
time: 201 us; the launch traced here: 200 us
  waiting for transfers between devices  69.4 us (35%)
  matrix products  47.1 us (23%)
  local copies, waits for them, and re-layouts  32.2 us (16%)
  blocking collectives  30.9 us (15%)
  between operations  13.9 us (7%)
  other arithmetic  6.01 us (3%)
    reduce_scatter x1, waiting for transfers between devices, body(): lax.psum_scatter(jnp.stack([gate_part, up_part, back_part], axis=1).astyp...  40.2 us
    unnamed x18, local copies, waits for them, and re-layouts  32.2 us
    all_gather x1, waiting for transfers between devices, body(): lax.all_gather(gate_loc, 'dp', axis=0, tiled=True)  16.1 us
    all_gather x1, blocking collectives, body(): lax.all_gather(incoming_entries, 'tensor', axis=0, tiled=True)  15.9 us
    all_gather x1, blocking collectives, body(): lax.all_gather(output_adjoint, 'tensor', axis=0, tiled=True)  15 us
    all_gather x1, waiting for transfers between devices, body(): lax.all_gather(up_loc, 'dp', axis=0, tiled=True)  11.9 us
    dot_general x1, matrix products, body(): lax.dot_general(up_grad, expansion_matrix, over_units, preferred_element_...  8.51 us
    dot_general x1, matrix products, body(): lax.dot_general(hidden, cot_all, over_rows, preferred_element_type=jnp.fl...  8.36 us
  transfers between devices with their start and end apart: 5, of which 3 were waited for; matrix products, arithmetic and copies ran while one was open for 34% of the time, Pallas kernels for 0%

commit v1 on v0

--- a/solution.py
+++ b/solution.py
@@ -1,8 +1,11 @@
+import functools
 import math
 
 import jax
 import jax.numpy as jnp
 from jax import lax
+from jax.experimental import pallas as pl
+from jax.experimental.pallas import tpu as pltpu
 from jax.sharding import PartitionSpec as P
 
 cubic_coef = 0.044715
@@ -29,7 +32,7 @@
     return (hidden, gate_grad, up_grad)
 
 
-def body(
+def plain_body(
     incoming_entries,
     output_adjoint,
     remaining_members,
@@ -83,7 +86,305 @@
     return (grad_tokens, grad_gate, grad_up, grad_down)
 
 
+MESH = pl.DeviceIdType.MESH
+NT = (((1,), (1,)), ((), ()))
+TN = (((0,), (0,)), ((), ()))
+
+
+def exchange_kernel(
+    n_z,
+    n_chunks,
+    tok_ref,
+    cot_ref,
+    members_ref,
+    wg_hbm,
+    wu_hbm,
+    wd_hbm,
+    tok_all,
+    cot_all,
+    h_all,
+    *rest,
+):
+    blocks = rest[:n_z]
+    (
+        wg, wu, wd, mine, csend, crecv, xsend, xrecv, acc,
+        w_sem, z_send, z_recv, c_send, c_recv, x_send, x_recv, h_send, h_recv,
+    ) = rest[n_z:]
+    rows = tok_ref.shape[0]
+    half = mine.shape[2]
+    width = wg.shape[2]
+    me_z = lax.axis_index("tensor")
+    me_d = lax.axis_index("dp")
+    core = lax.rem(me_d, 2)
+    other_core = me_d + 1 - 2 * core
+    other_chip = lax.rem(me_d + 2, 4)
+
+    def weight_copies(c):
+        cols = pl.ds(pl.multiple_of(c * width, width), width)
+        return (
+            pltpu.make_async_copy(wg_hbm.at[:, cols], wg.at[c], w_sem.at[0, c]),
+            pltpu.make_async_copy(wu_hbm.at[:, cols], wu.at[c], w_sem.at[1, c]),
+            pltpu.make_async_copy(wd_hbm.at[cols, :], wd.at[c], w_sem.at[2, c]),
+        )
+
+    @pl.loop(0, n_chunks)
+    def _(c):
+        for copy in weight_copies(c):
+            copy.start()
+
+    barrier = pltpu.get_barrier_semaphore()
+    for k in range(1, n_z):
+        pl.semaphore_signal(
+            barrier, inc=1, device_id={"tensor": lax.rem(me_z + k, n_z)}, device_id_type=MESH
+        )
+    pl.semaphore_signal(barrier, inc=1, device_id={"dp": other_core}, device_id_type=MESH)
+    pl.semaphore_signal(barrier, inc=1, device_id={"dp": other_chip}, device_id_type=MESH)
+    pl.semaphore_wait(barrier, n_z + 1)
+
+    own_rows = pl.ds(pl.multiple_of(me_z * rows, rows), rows)
+
+    def gather_copy(which, k):
+        src, dst = ((tok_ref, tok_all), (cot_ref, cot_all))[which]
+        return pltpu.make_async_remote_copy(
+            src_ref=src,
+            dst_ref=dst.at[own_rows, :],
+            send_sem=z_send.at[which, k - 1],
+            recv_sem=z_recv.at[which, k - 1],
+            device_id={"tensor": lax.rem(me_z + k, n_z)},
+            device_id_type=MESH,
+        )
+
+    for which in range(2):
+        for k in range(1, n_z):
+            gather_copy(which, k).start()
+    tok_all[own_rows, :] = tok_ref[...]
+    cot_all[own_rows, :] = cot_ref[...]
+    for which in range(2):
+        for k in range(1, n_z):
+            gather_copy(which, k).wait_recv()
+
+    def core_copy(c):
+        return pltpu.make_async_remote_copy(
+            src_ref=csend.at[c], dst_ref=crecv.at[c],
+            send_sem=c_send.at[c], recv_sem=c_recv.at[c],
+            device_id={"dp": other_core}, device_id_type=MESH,
+        )
+
+    def chip_copy(c):
+        return pltpu.make_async_remote_copy(
+            src_ref=xsend.at[c], dst_ref=xrecv.at[c],
+            send_sem=x_send.at[c], recv_sem=x_recv.at[c],
+            device_id={"dp": other_chip}, device_id_type=MESH,
+        )
+
+    kept = pl.ds(pl.multiple_of(core * half, half), half)
+    given = pl.ds(pl.multiple_of((1 - core) * half, half), half)
+
+    def hidden_copy(c):
+        return pltpu.make_async_remote_copy(
+            src_ref=h_all.at[c, :, kept, :], dst_ref=h_all.at[c, :, kept, :],
+            send_sem=h_send.at[c], recv_sem=h_recv.at[c],
+            device_id={"dp": other_core}, device_id_type=MESH,
+        )
+
+    def forward(c):
+        for copy in weight_copies(c):
+            copy.wait()
+        for j in range(3):
+            src = cot_all if j == 2 else tok_all
+            for dst, sel in ((csend, given), (mine, kept)):
+                lhs = src[sel, :]
+                if j == 2:
+                    out = lax.dot_general(lhs, wd[c], NT, preferred_element_type=jnp.float32)
+                else:
+                    out = jnp.dot(lhs, (wg, wu)[j][c], preferred_element_type=jnp.float32)
+                dst[c, j] = out.astype(dst.dtype)
+        core_copy(c).start()
+
+    def pair_sum(c):
+        core_copy(c).wait_recv()
+        xsend[c] = (mine[c] + crecv[c].astype(jnp.float32)).astype(xsend.dtype)
+        chip_copy(c).start()
+
+    @pl.loop(0, n_chunks)
+    def _(c):
+        forward(c)
+
+        @pl.when(c >= 1)
+        def _():
+            pair_sum(c - 1)
+
+    pair_sum(n_chunks - 1)
+
+    alive = jnp.float32(0.0)
+    for i in range(members_ref.shape[0]):
+        alive = alive + jnp.where(members_ref[i] == me_z, 1.0, 0.0).astype(jnp.float32)
+
+    def activate_chunk(c):
+        chip_copy(c).wait_recv()
+        step = 16
+        for r in range(0, half, step):
+            sums = [
+                xsend[c, j, r : r + step].astype(jnp.float32)
+                + xrecv[c, j, r : r + step].astype(jnp.float32)
+                for j in range(3)
+            ]
+            active, slope = gelu_pair(sums[0])
+            at = pl.ds(pl.multiple_of(core * half + r, step), step)
+            h_all[c, 0, at, :] = (alive * active * sums[1]).astype(h_all.dtype)
+            h_all[c, 1, at, :] = (alive * sums[2] * sums[1] * slope).astype(h_all.dtype)
+            h_all[c, 2, at, :] = (alive * sums[2] * active).astype(h_all.dtype)
+        hidden_copy(c).start()
+
+    def token_grad(c):
+        hidden_copy(c).wait_recv()
+        acc[...] += lax.dot_general(
+            h_all[c, 1], wg[c], NT, preferred_element_type=jnp.float32
+        ) + lax.dot_general(h_all[c, 2], wu[c], NT, preferred_element_type=jnp.float32)
+
+    acc[...] = jnp.zeros_like(acc)
+
+    @pl.loop(0, n_chunks)
+    def _(c):
+        activate_chunk(c)
+
+        @pl.when(c >= 1)
+        def _():
+            token_grad(c - 1)
+
+    token_grad(n_chunks - 1)
+    for k in range(n_z):
+        to = lax.rem(me_z + k, n_z)
+        blocks[k][...] = acc[pl.ds(pl.multiple_of(to * rows, rows), rows), :].astype(
+            blocks[k].dtype
+        )
+
+    for which in range(2):
+        for k in range(1, n_z):
+            gather_copy(which, k).wait_send()
+
+    @pl.loop(0, n_chunks)
+    def _(c):
+        core_copy(c).wait_send()
+        chip_copy(c).wait_send()
+        hidden_copy(c).wait_send()
+
+
+def exchange(tok, cot, members, wg, wu, wd, n_z, n_chunks):
+    rows, depth = tok.shape
+    units = wg.shape[1]
+    width = units // n_chunks
+    all_rows = rows * n_z
+    half = all_rows // 2
+    bf16, f32 = jnp.bfloat16, jnp.float32
+    vmem = pl.BlockSpec(memory_space=pltpu.VMEM)
+    hbm = pl.BlockSpec(memory_space=pl.ANY)
+    dma = pltpu.SemaphoreType.DMA
+    part = (n_chunks, 3, half, width)
+    return pl.pallas_call(
+        functools.partial(exchange_kernel, n_z, n_chunks),
+        out_shape=[
+            jax.ShapeDtypeStruct((all_rows, depth), bf16),
+            jax.ShapeDtypeStruct((all_rows, depth), bf16),
+            jax.ShapeDtypeStruct((n_chunks, 3, all_rows, width), bf16),
+            jax.ShapeDtypeStruct((rows, depth), f32),
+        ]
+        + [jax.ShapeDtypeStruct((rows, depth), bf16)] * (n_z - 1),
+        in_specs=[vmem, vmem, pl.BlockSpec(memory_space=pltpu.SMEM), hbm, hbm, hbm],
+        out_specs=[vmem] * (3 + n_z),
+        scratch_shapes=[
+            pltpu.VMEM((n_chunks, depth, width), bf16),
+            pltpu.VMEM((n_chunks, depth, width), bf16),
+            pltpu.VMEM((n_chunks, width, depth), bf16),
+            pltpu.VMEM(part, f32),
+            pltpu.VMEM(part, bf16),
+            pltpu.VMEM(part, bf16),
+            pltpu.VMEM(part, bf16),
+            pltpu.VMEM(part, bf16),
+            pltpu.VMEM((all_rows, depth), f32),
+            dma((3, n_chunks)),
+            dma((2, n_z - 1)),
+            dma((2, n_z - 1)),
+            dma((n_chunks,)),
+            dma((n_chunks,)),
+            dma((n_chunks,)),
+            dma((n_chunks,)),
+            dma((n_chunks,)),
+            dma((n_chunks,)),
+        ],
+        compiler_params=pltpu.CompilerParams(
+            collective_id=0, has_side_effects=True, vmem_limit_bytes=60 * 2**20
+        ),
+        cost_estimate=pl.CostEstimate(
+            flops=10 * all_rows * depth * units,
+            bytes_accessed=6 * depth * units,
+            transcendentals=half * units,
+        ),
+    )(tok, cot, members, wg, wu, wd)
+
+
+def weight_grads_kernel(tok_ref, cot_ref, h_ref, gate_ref, up_ref, down_ref, tok_t):
+    @pl.when(pl.program_id(0) == 0)
+    def _():
+        tok_t[...] = tok_ref[...].T
+
+    gate_ref[...] = jnp.dot(
+        tok_t[...], h_ref[0, 1], preferred_element_type=jnp.float32
+    ).astype(gate_ref.dtype)
+    up_ref[...] = jnp.dot(tok_t[...], h_ref[0, 2], preferred_element_type=jnp.float32).astype(
+        up_ref.dtype
+    )
+    down_ref[...] = lax.dot_general(
+        h_ref[0, 0], cot_ref[...], TN, preferred_element_type=jnp.float32
+    ).astype(down_ref.dtype)
+
+
+def weight_grads(tok_all, cot_all, h_all):
+    all_rows, depth = tok_all.shape
+    n_chunks, _, _, width = h_all.shape
+    units = n_chunks * width
+    bf16 = jnp.bfloat16
+    whole = pl.BlockSpec((all_rows, depth), lambda c: (0, 0))
+    return pl.pallas_call(
+        weight_grads_kernel,
+        grid=(n_chunks,),
+        out_shape=[
+            jax.ShapeDtypeStruct((depth, units), bf16),
+            jax.ShapeDtypeStruct((depth, units), bf16),
+            jax.ShapeDtypeStruct((units, depth), bf16),
+        ],
+        in_specs=[whole, whole, pl.BlockSpec((1, 3, all_rows, width), lambda c: (c, 0, 0, 0))],
+        out_specs=[
+            pl.BlockSpec((depth, width), lambda c: (0, c)),
+            pl.BlockSpec((depth, width), lambda c: (0, c)),
+            pl.BlockSpec((width, depth), lambda c: (c, 0)),
+        ],
+        scratch_shapes=[pltpu.VMEM((depth, all_rows), bf16)],
+        compiler_params=pltpu.CompilerParams(vmem_limit_bytes=40 * 2**20),
+        cost_estimate=pl.CostEstimate(
+            flops=6 * all_rows * depth * units,
+            bytes_accessed=6 * depth * units,
+            transcendentals=0,
+        ),
+    )(tok_all, cot_all, h_all)
+
+
+def fused_body(n_z, n_chunks, tok, cot, members, wg, wu, wd):
+    tok_all, cot_all, h_all, *blocks = exchange(tok, cot, members, wg, wu, wd, n_z, n_chunks)
+    arrived = [
+        lax.ppermute(blocks[k], "tensor", [(i, (i + k) % n_z) for i in range(n_z)])
+        for k in range(1, n_z)
+    ]
+    grad_gate, grad_up, grad_down = weight_grads(tok_all, cot_all, h_all)
+    total = blocks[0]
+    for block in arrived:
+        total = total + block.astype(jnp.float32)
+    return total.astype(jnp.bfloat16), grad_gate, grad_up, grad_down
+
+
 def solution(mesh):
+    n_z, n_dp = mesh.shape["tensor"], mesh.shape["dp"]
+    body = functools.partial(fused_body, n_z, 9) if n_dp == 4 and n_z == 4 else plain_body
     return jax.shard_map(
         body,
         mesh=mesh,

time: 201 us -> 88.5 us (0.44)
  Pallas kernels: 0 us -> 78.3 us
  waiting for transfers between devices: 69.4 us -> 0.01 us
  matrix products: 47.1 us -> 0 us
  blocking collectives: 30.9 us -> 0 us
  local copies, waits for them, and re-layouts: 32.2 us -> 3.93 us
  between operations: 13.9 us -> 0.66 us
  other arithmetic: 6.01 us -> 0.67 us
  starting transfers between devices: 0.38 us -> 4.66 us
    pallas_call x0 -> x2, Pallas kernels: none -> 78.3 us  [the longest x1 67.1 us: exchange(): pl.pallas_call(functools.partial(exchange_kernel, n_z, n_chunks), out_sha...]
    dot_general x8 -> x0, matrix products: 47.1 us -> none  [the longest x1 8.51 us: body(): lax.dot_general(up_grad, expansion_matrix, over_units, preferred_element_...]
    reduce_scatter x2 -> x0, waiting for transfers between devices: 40.2 us -> none  [the longest x1 40.2 us: body(): lax.psum_scatter(jnp.stack([gate_part, up_part, back_part], axis=1).astyp...]
    all_gather x2 -> x0, blocking collectives: 30.9 us -> none  [the longest x1 15.9 us: body(): lax.all_gather(incoming_entries, 'tensor', axis=0, tiled=True)]
    unnamed x18 -> x8, local copies, waits for them, and re-layouts: 32.2 us -> 3.93 us
    all_gather x3 -> x0, waiting for transfers between devices: 28 us -> none  [the longest x1 16.1 us: body(): lax.all_gather(gate_loc, 'dp', axis=0, tiled=True)]
    ppermute x0 -> x3, starting transfers between devices: none -> 4.66 us  [fused_body(): lax.ppermute(blocks[k], 'tensor', [(i, (i + k) % n_z) for i in range(n_z)])]
    convert_element_type x2 -> x1, other arithmetic: 3.4 us -> 0.67 us  [fused_body(): return (total.astype(jnp.bfloat16), grad_gate, grad_up, grad_down)]
  transfers between devices with their start and end apart: 5 -> 3, of which waited for: 3 -> 0; matrix products, arithmetic and copies ran while one was open for 34% -> 0% of each run, Pallas kernels for 0% -> 13%
where the time goes in v1:
time: 88.5 us; the launch traced here: 88.2 us
  Pallas kernels  78.3 us (88%)
  starting transfers between devices  4.66 us (5%)
  local copies, waits for them, and re-layouts  3.93 us (4%)
    pallas_call x1, Pallas kernels, exchange(): pl.pallas_call(functools.partial(exchange_kernel, n_z, n_chunks), out_sha...  67.1 us
    pallas_call x1, Pallas kernels, weight_grads(): pl.pallas_call(weight_grads_kernel, grid=(n_chunks,), out_shape=[jax.Shap...  11.3 us
    ppermute x3, starting transfers between devices, fused_body(): lax.ppermute(blocks[k], 'tensor', [(i, (i + k) % n_z) for i in range(n_z)])  4.66 us
    unnamed x8, local copies, waits for them, and re-layouts  3.93 us
  transfers between devices with their start and end apart: 3, of which 0 were waited for; matrix products, arithmetic and copies ran while one was open for 0% of the time, Pallas kernels for 13%

profile of v1, /device:TPU:0, one launch (start us, length us, event | category | flops | bytes accessed | tf_op | source)
XLA Modules:
  0.0 88.2 jit_solution(9440819699710250298)
XLA Ops:
  0.6 67.1 %shard_map.93 = (bf16[128,1152]{1,0:T(8,128)(2,1)}, bf16[128,1152]{1,0:T(8,128)(2,1)}, bf16[9,3,128,512]{3,2,1,0:T(8,128)(2,1)}, f32[32,1152]{1,0:T(8,128)}, bf1...) custom-call(bf16[32,1152]{1,0:T(8,128)(2,1)} %tok_ref.1, bf16[32,1152]{1,0:T(8,128)(2,1)} %cot_ref.1, ...), custom_call_target="tpu_custom_call" | custom-call | flops 6794772480 | bytes 31850496 | tf_op jit(solution)/shard_map/pallas_call | solution.py:284
  67.7 1.7 %collective-permute-start = (bf16[32,1152]{1,0:T(8,128)(2,1)}, bf16[32,1152]{1,0:T(8,128)(2,1)S(1)}, u32[]{:S(2)}, u32[]{:S(2)}) collective-permute-start(bf16[32,1152]{1,0:T(8,128)(2,1)} %get-tuple-element.15), channel_id=1, source_target_pairs={{0,4},{4,8},{8,12},{12,0},{1,5},{5,9},{9,13},{13,1},{2,6},{6,10},{... | collective-permute-start | bytes 221192 | tf_op jit(solution)/shard_map/ppermute | solution.py:375
  69.4 2.3 %collective-permute-start.1 = (bf16[32,1152]{1,0:T(8,128)(2,1)}, bf16[32,1152]{1,0:T(8,128)(2,1)S(1)}, u32[]{:S(2)}, u32[]{:S(2)}) collective-permute-start(bf16[32,1152]{1,0:T(8,128)(2,1)} %get-tuple-element.16), channel_id=1, source_target_pairs={{0,8},{4,12},{8,0},{12,4},{1,9},{5,13},{9,1},{13,5},{2,10},{6,14},... | collective-permute-start | bytes 221192 | tf_op jit(solution)/shard_map/ppermute | solution.py:375
  71.7 0.7 collective-permute-start.2
  72.4 0.0 copy-start
  72.4 2.0 %copy-done = bf16[9,3,128,512]{3,2,1,0:T(8,128)(2,1)S(1)} copy-done((bf16[9,3,128,512]{3,2,1,0:T(8,128)(2,1)S(1)}, bf16[9,3,128,512]{3,2,1,0:T(8,128)(2,1)}, u32[]{:S(2)}) %copy-start) | copy-done | bytes 3538968
  74.4 0.0 copy-start.1
  74.4 1.0 %copy-done.1 = bf16[128,1152]{1,0:T(8,128)(2,1)S(1)} copy-done((bf16[128,1152]{1,0:T(8,128)(2,1)S(1)}, bf16[128,1152]{1,0:T(8,128)(2,1)}, u32[]{:S(2)}) %copy-start.1) | copy-done | bytes 294936
  75.3 0.0 copy-start.2
  75.3 1.0 %copy-done.2 = bf16[128,1152]{1,0:T(8,128)(2,1)S(1)} copy-done((bf16[128,1152]{1,0:T(8,128)(2,1)S(1)}, bf16[128,1152]{1,0:T(8,128)(2,1)}, u32[]{:S(2)}) %copy-start.2) | copy-done | bytes 294936
  76.3 0.0 copy-start.3
  76.3 11.3 %shard_map.94 = (bf16[1152,4608]{1,0:T(8,128)(2,1)}, bf16[1152,4608]{1,0:T(8,128)(2,1)}, bf16[4608,1152]{1,0:T(8,128)(2,1)}) custom-call(bf16[128,1152]{1,0:T(8,128)(2,1)S(1)} %copy-done.1, bf16[128,1152]{1,0:T(8,128)(2,1)S(1)} %copy-done.2, bf16[9,3,128,512]{3,2,1,0:T(8,128)(2,1)S(1)} %copy-done), custom_call_target="tpu_custom_call" | custom-call | flops 4076863488 | bytes 31850496 | tf_op jit(solution)/shard_map/pallas_call | solution.py:348
  87.5 0.0 collective-permute-done
  87.5 0.0 collective-permute-done.1
  87.6 0.0 collective-permute-done.2
  87.6 0.0 copy-done.3
  87.6 0.7 add_convert_fusion
Async XLA Ops:
  67.7 19.9 %collective-permute-start = (bf16[32,1152]{1,0:T(8,128)(2,1)}, bf16[32,1152]{1,0:T(8,128)(2,1)S(1)}, u32[]{:S(2)}, u32[]{:S(2)}) collective-permute-start(bf16[32,1152]{1,0:T(8,128)(2,1)} %get-tuple-element.15), channel_id=1, source_target_pairs={{0,4},{4,8},{8,12},{12,0},{1,5},{5,9},{9,13},{13,1},{2,6},{6,10},{... | collective-permute-start | bytes 221192 | tf_op jit(solution)/shard_map/ppermute | solution.py:375
  69.4 18.2 %collective-permute-start.1 = (bf16[32,1152]{1,0:T(8,128)(2,1)}, bf16[32,1152]{1,0:T(8,128)(2,1)S(1)}, u32[]{:S(2)}, u32[]{:S(2)}) collective-permute-start(bf16[32,1152]{1,0:T(8,128)(2,1)} %get-tuple-element.16), channel_id=1, source_target_pairs={{0,8},{4,12},{8,0},{12,4},{1,9},{5,13},{9,1},{13,5},{2,10},{6,14},... | collective-permute-start | bytes 221192 | tf_op jit(solution)/shard_map/ppermute | solution.py:375
  71.7 15.9 %collective-permute-start.2 = (bf16[32,1152]{1,0:T(8,128)(2,1)}, bf16[32,1152]{1,0:T(8,128)(2,1)S(1)}, u32[]{:S(2)}, u32[]{:S(2)}) collective-permute-start(bf16[32,1152]{1,0:T(8,128)(2,1)} %get-tuple-element.17), channel_id=1, source_target_pairs={{0,12},{4,0},{8,4},{12,8},{1,13},{5,1},{9,5},{13,9},{2,14},{6,2},{... | collective-permute-start | bytes 221192 | tf_op jit(solution)/shard_map/ppermute | solution.py:375
  72.4 2.0 %copy-start = (bf16[9,3,128,512]{3,2,1,0:T(8,128)(2,1)S(1)}, bf16[9,3,128,512]{3,2,1,0:T(8,128)(2,1)}, u32[]{:S(2)}) copy-start(bf16[9,3,128,512]{3,2,1,0:T(8,128)(2,1)} %get-tuple-element.20.h_ref) | copy-start | bytes 10616836
  74.4 1.0 %copy-start.1 = (bf16[128,1152]{1,0:T(8,128)(2,1)S(1)}, bf16[128,1152]{1,0:T(8,128)(2,1)}, u32[]{:S(2)}) copy-start(bf16[128,1152]{1,0:T(8,128)(2,1)} %get-tuple-element.18.tok_ref) | copy-start | bytes 884740
  75.3 1.0 %copy-start.2 = (bf16[128,1152]{1,0:T(8,128)(2,1)S(1)}, bf16[128,1152]{1,0:T(8,128)(2,1)}, u32[]{:S(2)}) copy-start(bf16[128,1152]{1,0:T(8,128)(2,1)} %get-tuple-element.19.cot_ref) | copy-start | bytes 884740
  76.3 11.3 %copy-start.3 = (f32[32,1152]{1,0:T(8,128)S(1)}, f32[32,1152]{1,0:T(8,128)}, u32[]{:S(2)}) copy-start(f32[32,1152]{1,0:T(8,128)} %get-tuple-element.14) | copy-start | bytes 442372

commit v2 on v1

--- a/solution.py
+++ b/solution.py
@@ -141,7 +141,12 @@
     pl.semaphore_signal(barrier, inc=1, device_id={"dp": other_chip}, device_id_type=MESH)
     pl.semaphore_wait(barrier, n_z + 1)
 
-    own_rows = pl.ds(pl.multiple_of(me_z * rows, rows), rows)
+    def place(rank):
+        per_half = n_z // 2
+        slot = lax.rem(rank // per_half + core, 2) * per_half + lax.rem(rank, per_half)
+        return pl.ds(pl.multiple_of(slot * rows, rows), rows)
+
+    own_rows = place(me_z)
 
     def gather_copy(which, k):
         src, dst = ((tok_ref, tok_all), (cot_ref, cot_all))[which]
@@ -177,12 +182,9 @@
             device_id={"dp": other_chip}, device_id_type=MESH,
         )
 
-    kept = pl.ds(pl.multiple_of(core * half, half), half)
-    given = pl.ds(pl.multiple_of((1 - core) * half, half), half)
-
     def hidden_copy(c):
         return pltpu.make_async_remote_copy(
-            src_ref=h_all.at[c, :, kept, :], dst_ref=h_all.at[c, :, kept, :],
+            src_ref=h_all.at[c, :, :half, :], dst_ref=h_all.at[c, :, half:, :],
             send_sem=h_send.at[c], recv_sem=h_recv.at[c],
             device_id={"dp": other_core}, device_id_type=MESH,
         )
@@ -191,14 +193,14 @@
         for copy in weight_copies(c):
             copy.wait()
         for j in range(3):
-            src = cot_all if j == 2 else tok_all
-            for dst, sel in ((csend, given), (mine, kept)):
-                lhs = src[sel, :]
-                if j == 2:
-                    out = lax.dot_general(lhs, wd[c], NT, preferred_element_type=jnp.float32)
-                else:
-                    out = jnp.dot(lhs, (wg, wu)[j][c], preferred_element_type=jnp.float32)
-                dst[c, j] = out.astype(dst.dtype)
+            if j == 2:
+                out = lax.dot_general(
+                    cot_all[...], wd[c], NT, preferred_element_type=jnp.float32
+                )
+            else:
+                out = jnp.dot(tok_all[...], (wg, wu)[j][c], preferred_element_type=jnp.float32)
+            mine[c, j] = out[:half]
+            csend[c, j] = out[half:].astype(csend.dtype)
         core_copy(c).start()
 
     def pair_sum(c):
@@ -230,7 +232,7 @@
                 for j in range(3)
             ]
             active, slope = gelu_pair(sums[0])
-            at = pl.ds(pl.multiple_of(core * half + r, step), step)
+            at = slice(r, r + step)
             h_all[c, 0, at, :] = (alive * active * sums[1]).astype(h_all.dtype)
             h_all[c, 1, at, :] = (alive * sums[2] * sums[1] * slope).astype(h_all.dtype)
             h_all[c, 2, at, :] = (alive * sums[2] * active).astype(h_all.dtype)
@@ -255,7 +257,7 @@
     token_grad(n_chunks - 1)
     for k in range(n_z):
         to = lax.rem(me_z + k, n_z)
-        blocks[k][...] = acc[pl.ds(pl.multiple_of(to * rows, rows), rows), :].astype(
+        blocks[k][...] = acc[place(to), :].astype(
             blocks[k].dtype
         )
 
@@ -360,7 +362,7 @@
             pl.BlockSpec((width, depth), lambda c: (c, 0)),
         ],
         scratch_shapes=[pltpu.VMEM((depth, all_rows), bf16)],
-        compiler_params=pltpu.CompilerParams(vmem_limit_bytes=40 * 2**20),
+        compiler_params=pltpu.CompilerParams(vmem_limit_bytes=60 * 2**20),
         cost_estimate=pl.CostEstimate(
             flops=6 * all_rows * depth * units,
             bytes_accessed=6 * depth * units,

time: 88.5 us -> 86 us (0.972)
  local copies, waits for them, and re-layouts: 3.93 us -> 0.01 us
  Pallas kernels: 78.3 us -> 79.6 us
    unnamed x8 -> x2, local copies, waits for them, and re-layouts: 3.93 us -> 0.01 us
    pallas_call x1, Pallas kernels: 11.3 us -> 13.3 us  [weight_grads(): pl.pallas_call(weight_grads_kernel, grid=(n_chunks,), out_shape=[jax.Shap...]
  transfers between devices with their start and end apart: 3 -> 3, of which waited for: 0 -> 0; matrix products, arithmetic and copies ran while one was open for 0% -> 0% of each run, Pallas kernels for 13% -> 16%
where the time goes in v2:
time: 86 us; the launch traced here: 85.6 us
  Pallas kernels  79.6 us (93%)
  starting transfers between devices  4.67 us (5%)
    pallas_call x1, Pallas kernels, exchange(): pl.pallas_call(functools.partial(exchange_kernel, n_z, n_chunks), out_sha...  66.3 us
    pallas_call x1, Pallas kernels, weight_grads(): pl.pallas_call(weight_grads_kernel, grid=(n_chunks,), out_shape=[jax.Shap...  13.3 us
    ppermute x3, starting transfers between devices, fused_body(): lax.ppermute(blocks[k], 'tensor', [(i, (i + k) % n_z) for i in range(n_z)])  4.67 us
  transfers between devices with their start and end apart: 3, of which 0 were waited for; matrix products, arithmetic and copies ran while one was open for 0% of the time, Pallas kernels for 16%

profile of v2, /device:TPU:0, one launch (start us, length us, event | category | flops | bytes accessed | tf_op | source)
XLA Modules:
  0.0 85.6 jit_solution(6945254163644791969)
XLA Ops:
  0.6 66.3 %shard_map.93 = (bf16[128,1152]{1,0:T(8,128)(2,1)}, bf16[128,1152]{1,0:T(8,128)(2,1)}, bf16[9,3,128,512]{3,2,1,0:T(8,128)(2,1)}, f32[32,1152]{1,0:T(8,128)}, bf1...) custom-call(bf16[32,1152]{1,0:T(8,128)(2,1)} %tok_ref.1, bf16[32,1152]{1,0:T(8,128)(2,1)} %cot_ref.1, ...), custom_call_target="tpu_custom_call" | custom-call | flops 6794772480 | bytes 31850496 | tf_op jit(solution)/shard_map/pallas_call | solution.py:286
  66.9 0.0 copy-start
  67.0 1.7 %collective-permute-start = (bf16[32,1152]{1,0:T(8,128)(2,1)}, bf16[32,1152]{1,0:T(8,128)(2,1)S(1)}, u32[]{:S(2)}, u32[]{:S(2)}) collective-permute-start(bf16[32,1152]{1,0:T(8,128)(2,1)} %get-tuple-element.15), channel_id=1, source_target_pairs={{0,4},{4,8},{8,12},{12,0},{1,5},{5,9},{9,13},{13,1},{2,6},{6,10},{... | collective-permute-start | bytes 221192 | tf_op jit(solution)/shard_map/ppermute | solution.py:377
  68.6 2.3 %collective-permute-start.1 = (bf16[32,1152]{1,0:T(8,128)(2,1)}, bf16[32,1152]{1,0:T(8,128)(2,1)S(1)}, u32[]{:S(2)}, u32[]{:S(2)}) collective-permute-start(bf16[32,1152]{1,0:T(8,128)(2,1)} %get-tuple-element.16), channel_id=1, source_target_pairs={{0,8},{4,12},{8,0},{12,4},{1,9},{5,13},{9,1},{13,5},{2,10},{6,14},... | collective-permute-start | bytes 221192 | tf_op jit(solution)/shard_map/ppermute | solution.py:377
  71.0 0.7 collective-permute-start.2
  71.6 13.3 %shard_map.94 = (bf16[1152,4608]{1,0:T(8,128)(2,1)}, bf16[1152,4608]{1,0:T(8,128)(2,1)}, bf16[4608,1152]{1,0:T(8,128)(2,1)}) custom-call(bf16[128,1152]{1,0:T(8,128)(2,1)} %get-tuple-element.18.tok_ref, bf16[128,1152]{1,0:T(8,128)(2,1)} %get-tuple-element.19.cot_ref, bf16[9,3,128,512]{3,2,1,0:T(8,128)(2,1)} %get-tuple-element.20.h_ref), custom_call_target="tpu_custom_call" | custom-call | flops 4076863488 | bytes 31850496 | tf_op jit(solution)/shard_map/pallas_call | solution.py:350
  84.9 0.0 collective-permute-done
  84.9 0.0 collective-permute-done.1
  84.9 0.0 collective-permute-done.2
  84.9 0.0 copy-done
  84.9 0.7 add_convert_fusion
Async XLA Ops:
  66.9 18.0 %copy-start = (f32[32,1152]{1,0:T(8,128)S(1)}, f32[32,1152]{1,0:T(8,128)}, u32[]{:S(2)}) copy-start(f32[32,1152]{1,0:T(8,128)} %get-tuple-element.14) | copy-start | bytes 442372
  67.0 18.0 %collective-permute-start = (bf16[32,1152]{1,0:T(8,128)(2,1)}, bf16[32,1152]{1,0:T(8,128)(2,1)S(1)}, u32[]{:S(2)}, u32[]{:S(2)}) collective-permute-start(bf16[32,1152]{1,0:T(8,128)(2,1)} %get-tuple-element.15), channel_id=1, source_target_pairs={{0,4},{4,8},{8,12},{12,0},{1,5},{5,9},{9,13},{13,1},{2,6},{6,10},{... | collective-permute-start | bytes 221192 | tf_op jit(solution)/shard_map/ppermute | solution.py:377
  68.6 16.3 %collective-permute-start.1 = (bf16[32,1152]{1,0:T(8,128)(2,1)}, bf16[32,1152]{1,0:T(8,128)(2,1)S(1)}, u32[]{:S(2)}, u32[]{:S(2)}) collective-permute-start(bf16[32,1152]{1,0:T(8,128)(2,1)} %get-tuple-element.16), channel_id=1, source_target_pairs={{0,8},{4,12},{8,0},{12,4},{1,9},{5,13},{9,1},{13,5},{2,10},{6,14},... | collective-permute-start | bytes 221192 | tf_op jit(solution)/shard_map/ppermute | solution.py:377
  71.0 14.0 %collective-permute-start.2 = (bf16[32,1152]{1,0:T(8,128)(2,1)}, bf16[32,1152]{1,0:T(8,128)(2,1)S(1)}, u32[]{:S(2)}, u32[]{:S(2)}) collective-permute-start(bf16[32,1152]{1,0:T(8,128)(2,1)} %get-tuple-element.17), channel_id=1, source_target_pairs={{0,12},{4,0},{8,4},{12,8},{1,13},{5,1},{9,5},{13,9},{2,14},{6,2},{... | collective-permute-start | bytes 221192 | tf_op jit(solution)/shard_map/ppermute | solution.py:377
